TPU v7x, 512 devices: a whole 4x8x8 slice. The times are simulated.
512 devices in a mesh: space: 64 (over y, z_hi, core), chan: 8 (over x, z_lo).
Axes of the slice: x: 4, y: 8, z: 8 (z_hi: 4, z_lo: 2; z = z_hi * 2 + z_lo), core: 2. Of those that a mesh axis runs over, the one named last changes fastest.
Arguments:
- blocks: bfloat16 [512, 4, 4, 4, 128], P(('space', 'chan')), may hold values from -6 to 6
- kernel_one: bfloat16 [3, 3, 3, 128, 256], replicated, may hold values from -0.109375 to 0.109375
- bias_one: float32 [256], replicated, may hold values from -3 to 3
- kernel_two: bfloat16 [3, 3, 3, 256, 256], P(None, None, None, None, 'chan'), may hold values from -0.078125 to 0.078125
- bias_two: float32 [256], P('chan'), may hold values from -3 to 3
Outputs:
- features: bfloat16 [64, 8, 8, 8, 256], P('space', None, None, None, 'chan')
All inputs are finite; a program needn't handle non-finite values.
Results may differ from a plain program's by a relative error of at most 0.0045.
Values may be sent and summed in bfloat16 or wider, within the bound.
A program may use at most 64 MiB of HBM per device.

v0:
```python
import jax
import jax.numpy as jnp
from jax import lax
from jax.sharding import PartitionSpec as P

GY = 4
GZ = 4


def shifted(x, axis, by):
    size = lax.axis_size(axis)
    pairs = [(i, i + by) for i in range(size) if 0 <= i + by < size]
    return lax.ppermute(x, axis, pairs)


def widen(tile, dim, stride, count):
    where = lax.axis_index("space") // stride % count
    length = tile.shape[dim]
    planes = []
    for sign in (1, -1):
        start = length - 1 if sign == 1 else 0
        plane = lax.slice_in_dim(tile, start, start + 1, 1, dim)
        got = shifted(plane, "space", sign * stride)
        keep = (
            jnp.where(where > 0, 1.0, 0.0) if sign == 1 else jnp.where(where < count - 1, 1.0, 0.0)
        )
        planes.append(got * keep.astype(got.dtype))
    return jnp.concatenate([planes[0], tile, planes[1]], axis=dim)


def with_rim(tile):
    along_x = lax.axis_size("space") // (GY * GZ)
    padded = widen(tile, 2, 1, GZ)
    padded = widen(padded, 1, GZ, GY)
    return widen(padded, 0, GY * GZ, along_x)


def convolve_valid(padded, kernel, layout):
    return lax.conv_general_dilated(
        padded[None],
        kernel,
        (1, 1, 1),
        "VALID",
        dimension_numbers=("NDHWC", "DHWIO", layout),
        preferred_element_type=jnp.float32,
    )


def taps_sum(carry, padded, kernel):
    return carry + convolve_valid(padded, kernel, "NDHWC").reshape(carry.shape)


def on_device(blocks, kernel_one, bias_one, kernel_two, bias_two):
    mine = lax.axis_index("chan")
    groups = lax.axis_size("chan")
    filters_two = kernel_two.shape[4]
    moved = lax.all_to_all(blocks, "chan", split_axis=4, concat_axis=0, tiled=True)
    half = moved.shape[1]
    width = 2 * half
    shard = moved.shape[4]
    tile = (
        moved.reshape(2, 2, 2, half, half, half, shard)
        .transpose(0, 3, 1, 4, 2, 5, 6)
        .reshape(width, width, width, shard)
    )
    filters_one = kernel_one.shape[4] // groups
    bias_mine = lax.dynamic_slice_in_dim(bias_one, mine * filters_one, filters_one, 0)
    padded = with_rim(tile)
    kernel_mine = lax.dynamic_slice_in_dim(kernel_one, mine * filters_one, filters_one, 4)
    empty = jnp.zeros((width * width * width, filters_one), jnp.float32)
    total = taps_sum(empty, lax.all_gather(padded, "chan", axis=3, tiled=True), kernel_mine)
    hidden = jnp.maximum(total + bias_mine, 0.0).astype(jnp.bfloat16)
    hidden = hidden.reshape(width, width, width, filters_one)
    empty_two = jnp.zeros((width * width * width, filters_two), jnp.float32)
    whole = lax.all_gather(hidden, "chan", axis=3, tiled=True)
    total_two = taps_sum(empty_two, with_rim(whole), kernel_two)
    output = jnp.maximum(total_two + bias_two, 0.0).astype(jnp.bfloat16)
    return output.reshape(1, width, width, width, filters_two)


def solution(mesh):
    placed = (
        P(("space", "chan"), None, None, None, None),
        P(),
        P(),
        P(None, None, None, None, "chan"),
        P("chan"),
    )
    return jax.shard_map(
        on_device,
        mesh=mesh,
        in_specs=placed,
        out_specs=P("space", None, None, None, "chan"),
        check_vma=False,
    )
```

profile of v0, /device:TPU:1, one launch (start us, length us, event | category | flops | bytes accessed | tf_op | source)
XLA Modules:
  0.0 305.4 jit_solution(12990513578872300640)
XLA Ops:
  0.0 1.3 copy.43
  2.1 11.5 %all_to_all.15 = bf16[8,2,512]{2,1,0:T(2,128)(2,1)S(1)} all-to-all(bf16[8,2,512]{2,1,0:T(2,128)(2,1)S(1)} %reshape.29), channel_id=1, replica_groups=mesh['space'=64,'chan'=8] {'chan'}, dimensions={0} | all-to-all | bytes 32768 | tf_op jit(solution)/shard_map/all_to_all | solution.py:57
  15.8 7.8 %collective-permute-start = (bf16[8,8,1,16]{3,2,1,0:T(2,128)(2,1)S(1)}, bf16[8,8,1,16]{3,2,1,0:T(2,128)(2,1)S(1)}, u32[]{:S(2)}, u32[]{:S(2)}) collective-permute-start(bf16[8,8,1,16]{3,2,1,0:T(2,128)(2,1)S(1)} %get-tuple-element.15), channel_id=1, source_target_pairs={{0,8},{8,16},{16,24},{24,32},{32,40},{40,48},{48,56},{56,64},{64,7... | collective-permute-start | bytes 6152 | tf_op jit(solution)/shard_map/ppermute | solution.py:13
  23.7 1.9 collective-permute-start.1
  25.7 4.5 %collective-permute-done.1 = bf16[8,8,1,16]{3,2,1,0:T(2,128)(2,1)S(1)} collective-permute-done((bf16[8,8,1,16]{3,2,1,0:T(2,128)(2,1)S(1)}, bf16[8,8,1,16]{3,2,1,0:T(2,128)(2,1)S(1)}, u32[]{:S(2)}, u32[]{:S(2)}) %collective-permute-start.1) | collective-permute-done | bytes 2080 | tf_op jit(solution)/shard_map/ppermute | solution.py:13
  30.3 7.8 %collective-permute-start.2 = (bf16[8,1,10,16]{3,2,1,0:T(8,128)(2,1)S(1)}, bf16[8,1,10,16]{3,2,1,0:T(8,128)(2,1)S(1)}, u32[]{:S(2)}, u32[]{:S(2)}) collective-permute-start(bf16[8,1,10,16]{3,2,1,0:T(8,128)(2,1)S(1)} %get-tuple-element.13), channel_id=1, source_target_pairs={{0,32},{8,40},{16,48},{24,56},{32,64},{40,72},{48,80},{56,88},{64,... | collective-permute-start | bytes 7688 | tf_op jit(solution)/shard_map/ppermute | solution.py:13
  38.1 1.3 collective-permute-start.3
  39.5 7.8 %collective-permute-done.3 = bf16[8,1,10,16]{3,2,1,0:T(8,128)(2,1)S(1)} collective-permute-done((bf16[8,1,10,16]{3,2,1,0:T(8,128)(2,1)S(1)}, bf16[8,1,10,16]{3,2,1,0:T(8,128)(2,1)S(1)}, u32[]{:S(2)}, u32[]{:S(2)}) %collective-permute-start.3) | collective-permute-done | bytes 2592 | tf_op jit(solution)/shard_map/ppermute | solution.py:13
  47.3 4.2 %collective-permute-start.4 = (bf16[1,10,10,16]{3,2,1,0:T(8,128)(2,1)S(1)}, bf16[1,10,10,16]{3,2,1,0:T(8,128)(2,1)S(1)}, u32[]{:S(2)}, u32[]{:S(2)}) collective-permute-start(bf16[1,10,10,16]{3,2,1,0:T(8,128)(2,1)S(1)} %get-tuple-element.11), channel_id=1, source_target_pairs={{0,128},{8,136},{16,144},{24,152},{32,160},{40,168},{48,176},{56,1... | collective-permute-start | bytes 9608 | tf_op jit(solution)/shard_map/ppermute | solution.py:13
  53.0 6.4 %collective-permute-done.5 = bf16[1,10,10,16]{3,2,1,0:T(8,128)(2,1)S(1)} collective-permute-done((bf16[1,10,10,16]{3,2,1,0:T(8,128)(2,1)S(1)}, bf16[1,10,10,16]{3,2,1,0:T(8,128)(2,1)S(1)}, u32[]{:S(2)}, u32[]{:S(2)}) %collective-permute-start.5) | collective-permute-done | bytes 3232 | tf_op jit(solution)/shard_map/ppermute | solution.py:13
  60.8 100.4 %all_gather.6 = bf16[10,10,10,128]{2,1,0,3:T(8,128)(2,1)} all-gather(bf16[10,10,10,16]{2,1,0,3:T(8,128)(2,1)S(1)} %copy.46), channel_id=1, replica_groups=mesh['space'=64,'chan'=8] {'chan'}, dimensions={3}, use_global_device_ids=true | all-gather | bytes 288000 | tf_op jit(solution)/shard_map/all_gather | solution.py:71
  161.2 7.5 %copy.49 = bf16[1,10,10,10,128]{4,0,3,2,1:T(2,128)(2,1)S(1)} copy(bf16[1,10,10,10,128]{3,2,1,4,0:T(8,128)(2,1)} %bitcast.16) | data formatting | bytes 512000 | tf_op jit(solution)/shard_map/broadcast_in_dim | solution.py:40
  168.7 2.9 fusion.2
  172.5 80.0 %all_gather.7 = bf16[8,8,8,256]{2,1,0,3:T(8,128)(2,1)} all-gather(bf16[8,8,8,32]{2,1,0,3:T(8,128)(2,1)S(1)} %copy.50), channel_id=1, replica_groups=mesh['space'=64,'chan'=8] {'chan'}, dimensions={3}, use_global_device_ids=true | all-gather | bytes 294912 | tf_op jit(solution)/shard_map/all_gather | solution.py:75
  252.6 4.8 %copy.51 = bf16[8,8,8,256]{3,2,1,0:T(8,128)(2,1)S(1)} copy(bf16[8,8,8,256]{2,1,0,3:T(8,128)(2,1)} %all_gather.7) | data formatting | bytes 524288 | tf_op jit(solution)/shard_map/all_gather | solution.py:75
  257.5 6.3 %collective-permute-start.6 = (bf16[8,8,1,256]{3,2,1,0:T(2,128)(2,1)S(1)}, bf16[8,8,1,256]{3,2,1,0:T(2,128)(2,1)S(1)}, u32[]{:S(2)}, u32[]{:S(2)}) collective-permute-start(bf16[8,8,1,256]{3,2,1,0:T(2,128)(2,1)S(1)} %get-tuple-element.9), channel_id=1, source_target_pairs={{0,8},{8,16},{16,24},{24,32},{32,40},{40,48},{48,56},{56,64},{64,7... | collective-permute-start | bytes 98312 | tf_op jit(solution)/shard_map/ppermute | solution.py:13
  263.8 1.9 collective-permute-start.7
  265.8 4.5 %collective-permute-done.7 = bf16[8,8,1,256]{3,2,1,0:T(2,128)(2,1)S(1)} collective-permute-done((bf16[8,8,1,256]{3,2,1,0:T(2,128)(2,1)S(1)}, bf16[8,8,1,256]{3,2,1,0:T(2,128)(2,1)S(1)}, u32[]{:S(2)}, u32[]{:S(2)}) %collective-permute-start.7) | collective-permute-done | bytes 32800 | tf_op jit(solution)/shard_map/ppermute | solution.py:13
  270.5 5.6 %collective-permute-start.8 = (bf16[8,1,10,256]{3,2,1,0:T(8,128)(2,1)S(1)}, bf16[8,1,10,256]{3,2,1,0:T(8,128)(2,1)S(1)}, u32[]{:S(2)}, u32[]{:S(2)}) collective-permute-start(bf16[8,1,10,256]{3,2,1,0:T(8,128)(2,1)S(1)} %get-tuple-element.7), channel_id=1, source_target_pairs={{0,32},{8,40},{16,48},{24,56},{32,64},{40,72},{48,80},{56,88},{64,... | collective-permute-start | bytes 122888 | tf_op jit(solution)/shard_map/ppermute | solution.py:13
  277.4 7.6 %collective-permute-done.9 = bf16[8,1,10,256]{3,2,1,0:T(8,128)(2,1)S(1)} collective-permute-done((bf16[8,1,10,256]{3,2,1,0:T(8,128)(2,1)S(1)}, bf16[8,1,10,256]{3,2,1,0:T(8,128)(2,1)S(1)}, u32[]{:S(2)}, u32[]{:S(2)}) %collective-permute-start.9) | collective-permute-done | bytes 40992 | tf_op jit(solution)/shard_map/ppermute | solution.py:13
  285.1 5.5 %collective-permute-start.10 = (bf16[1,10,10,256]{3,2,1,0:T(8,128)(2,1)S(1)}, bf16[1,10,10,256]{3,2,1,0:T(8,128)(2,1)S(1)}, u32[]{:S(2)}, u32[]{:S(2)}) collective-permute-start(bf16[1,10,10,256]{3,2,1,0:T(8,128)(2,1)S(1)} %get-tuple-element.5), channel_id=1, source_target_pairs={{0,128},{8,136},{16,144},{24,152},{32,160},{40,168},{48,176},{56,1... | collective-permute-start | bytes 153608 | tf_op jit(solution)/shard_map/ppermute | solution.py:13
  290.6 1.5 collective-permute-start.11
  292.1 7.0 %collective-permute-done.11 = bf16[1,10,10,256]{3,2,1,0:T(8,128)(2,1)S(1)} collective-permute-done((bf16[1,10,10,256]{3,2,1,0:T(8,128)(2,1)S(1)}, bf16[1,10,10,256]{3,2,1,0:T(8,128)(2,1)S(1)}, u32[]{:S(2)}, u32[]{:S(2)}) %collective-permute-start.11) | collective-permute-done | bytes 51232 | tf_op jit(solution)/shard_map/ppermute | solution.py:13
  299.5 5.2 %fusion = f32[1,8,8,8,32]{4,0,3,2,1:T(1,128)S(1)} fusion(bf16[3,3,3,256,32]{3,4,2,1,0:T(8,128)(2,1)S(1)} %copy-done.2, bf16[1,10,10,10,256]{4,3,2,1,0:T(8,128)(2,1)S(1)} %maximum_bitcast_fusion), kind=kOutput, calls=%fused_computation | convolution fusion | flops 226492416 | bytes 1019904 | tf_op jit(solution)/shard_map/conv_general_dilated | solution.py:39
  (45 shorter events, 9.7 us)
Async XLA Ops:
  0.0 168.7 %copy-start = (bf16[3,3,3,128,256]{4,3,2,1,0:T(8,128)(2,1)S(1)}, bf16[3,3,3,128,256]{4,3,2,1,0:T(8,128)(2,1)}, u32[]{:S(2)}) copy-start(bf16[3,3,3,128,256]{4,3,2,1,0:T(8,128)(2,1)} %param.6) | copy-start | bytes 5308420
  1.3 50.3 %copy-start.3 = (f32[256]{0:T(256)S(1)}, f32[256]{0:T(256)}, u32[]{:S(2)}) copy-start(f32[256]{0:T(256)} %param.7) | copy-start | bytes 3076
  15.8 9.8 %collective-permute-start = (bf16[8,8,1,16]{3,2,1,0:T(2,128)(2,1)S(1)}, bf16[8,8,1,16]{3,2,1,0:T(2,128)(2,1)S(1)}, u32[]{:S(2)}, u32[]{:S(2)}) collective-permute-start(bf16[8,8,1,16]{3,2,1,0:T(2,128)(2,1)S(1)} %get-tuple-element.15), channel_id=1, source_target_pairs={{0,8},{8,16},{16,24},{24,32},{32,40},{40,48},{48,56},{56,64},{64,7... | collective-permute-start | bytes 6152 | tf_op jit(solution)/shard_map/ppermute | solution.py:13
  23.7 6.5 %collective-permute-start.1 = (bf16[8,8,1,16]{3,2,1,0:T(2,128)(2,1)S(1)}, bf16[8,8,1,16]{3,2,1,0:T(2,128)(2,1)S(1)}, u32[]{:S(2)}, u32[]{:S(2)}) collective-permute-start(bf16[8,8,1,16]{3,2,1,0:T(2,128)(2,1)S(1)} %get-tuple-element.16), channel_id=1, source_target_pairs={{8,0},{16,8},{24,16},{32,24},{40,32},{48,40},{56,48},{64,56},{72,6... | collective-permute-start | bytes 6152 | tf_op jit(solution)/shard_map/ppermute | solution.py:13
  30.3 9.2 %collective-permute-start.2 = (bf16[8,1,10,16]{3,2,1,0:T(8,128)(2,1)S(1)}, bf16[8,1,10,16]{3,2,1,0:T(8,128)(2,1)S(1)}, u32[]{:S(2)}, u32[]{:S(2)}) collective-permute-start(bf16[8,1,10,16]{3,2,1,0:T(8,128)(2,1)S(1)} %get-tuple-element.13), channel_id=1, source_target_pairs={{0,32},{8,40},{16,48},{24,56},{32,64},{40,72},{48,80},{56,88},{64,... | collective-permute-start | bytes 7688 | tf_op jit(solution)/shard_map/ppermute | solution.py:13
  38.1 9.1 %collective-permute-start.3 = (bf16[8,1,10,16]{3,2,1,0:T(8,128)(2,1)S(1)}, bf16[8,1,10,16]{3,2,1,0:T(8,128)(2,1)S(1)}, u32[]{:S(2)}, u32[]{:S(2)}) collective-permute-start(bf16[8,1,10,16]{3,2,1,0:T(8,128)(2,1)S(1)} %get-tuple-element.14), channel_id=1, source_target_pairs={{32,0},{40,8},{48,16},{56,24},{64,32},{72,40},{80,48},{88,56},{96,... | collective-permute-start | bytes 7688 | tf_op jit(solution)/shard_map/ppermute | solution.py:13
  47.3 5.7 %collective-permute-start.4 = (bf16[1,10,10,16]{3,2,1,0:T(8,128)(2,1)S(1)}, bf16[1,10,10,16]{3,2,1,0:T(8,128)(2,1)S(1)}, u32[]{:S(2)}, u32[]{:S(2)}) collective-permute-start(bf16[1,10,10,16]{3,2,1,0:T(8,128)(2,1)S(1)} %get-tuple-element.11), channel_id=1, source_target_pairs={{0,128},{8,136},{16,144},{24,152},{32,160},{40,168},{48,176},{56,1... | collective-permute-start | bytes 9608 | tf_op jit(solution)/shard_map/ppermute | solution.py:13
  51.7 7.7 %collective-permute-start.5 = (bf16[1,10,10,16]{3,2,1,0:T(8,128)(2,1)S(1)}, bf16[1,10,10,16]{3,2,1,0:T(8,128)(2,1)S(1)}, u32[]{:S(2)}, u32[]{:S(2)}) collective-permute-start(bf16[1,10,10,16]{3,2,1,0:T(8,128)(2,1)S(1)} %get-tuple-element.12), channel_id=1, source_target_pairs={{128,0},{136,8},{144,16},{152,24},{160,32},{168,40},{176,48},{184,... | collective-permute-start | bytes 9608 | tf_op jit(solution)/shard_map/ppermute | solution.py:13
  257.5 8.3 %collective-permute-start.6 = (bf16[8,8,1,256]{3,2,1,0:T(2,128)(2,1)S(1)}, bf16[8,8,1,256]{3,2,1,0:T(2,128)(2,1)S(1)}, u32[]{:S(2)}, u32[]{:S(2)}) collective-permute-start(bf16[8,8,1,256]{3,2,1,0:T(2,128)(2,1)S(1)} %get-tuple-element.9), channel_id=1, source_target_pairs={{0,8},{8,16},{16,24},{24,32},{32,40},{40,48},{48,56},{56,64},{64,7... | collective-permute-start | bytes 98312 | tf_op jit(solution)/shard_map/ppermute | solution.py:13
  263.8 6.5 %collective-permute-start.7 = (bf16[8,8,1,256]{3,2,1,0:T(2,128)(2,1)S(1)}, bf16[8,8,1,256]{3,2,1,0:T(2,128)(2,1)S(1)}, u32[]{:S(2)}, u32[]{:S(2)}) collective-permute-start(bf16[8,8,1,256]{3,2,1,0:T(2,128)(2,1)S(1)} %get-tuple-element.10), channel_id=1, source_target_pairs={{8,0},{16,8},{24,16},{32,24},{40,32},{48,40},{56,48},{64,56},{72,6... | collective-permute-start | bytes 98312 | tf_op jit(solution)/shard_map/ppermute | solution.py:13
  270.4 29.1 %copy-start.2 = (bf16[3,3,3,256,32]{3,4,2,1,0:T(8,128)(2,1)S(1)}, bf16[3,3,3,256,32]{3,4,2,1,0:T(8,128)(2,1)}, u32[]{:S(2)}) copy-start(bf16[3,3,3,256,32]{3,4,2,1,0:T(8,128)(2,1)} %param.8) | copy-start | bytes 1327108
  270.5 6.9 %collective-permute-start.8 = (bf16[8,1,10,256]{3,2,1,0:T(8,128)(2,1)S(1)}, bf16[8,1,10,256]{3,2,1,0:T(8,128)(2,1)S(1)}, u32[]{:S(2)}, u32[]{:S(2)}) collective-permute-start(bf16[8,1,10,256]{3,2,1,0:T(8,128)(2,1)S(1)} %get-tuple-element.7), channel_id=1, source_target_pairs={{0,32},{8,40},{16,48},{24,56},{32,64},{40,72},{48,80},{56,88},{64,... | collective-permute-start | bytes 122888 | tf_op jit(solution)/shard_map/ppermute | solution.py:13
  276.1 8.9 %collective-permute-start.9 = (bf16[8,1,10,256]{3,2,1,0:T(8,128)(2,1)S(1)}, bf16[8,1,10,256]{3,2,1,0:T(8,128)(2,1)S(1)}, u32[]{:S(2)}, u32[]{:S(2)}) collective-permute-start(bf16[8,1,10,256]{3,2,1,0:T(8,128)(2,1)S(1)} %get-tuple-element.8), channel_id=1, source_target_pairs={{32,0},{40,8},{48,16},{56,24},{64,32},{72,40},{80,48},{88,56},{96,... | collective-permute-start | bytes 122888 | tf_op jit(solution)/shard_map/ppermute | solution.py:13
  285.1 7.0 %collective-permute-start.10 = (bf16[1,10,10,256]{3,2,1,0:T(8,128)(2,1)S(1)}, bf16[1,10,10,256]{3,2,1,0:T(8,128)(2,1)S(1)}, u32[]{:S(2)}, u32[]{:S(2)}) collective-permute-start(bf16[1,10,10,256]{3,2,1,0:T(8,128)(2,1)S(1)} %get-tuple-element.5), channel_id=1, source_target_pairs={{0,128},{8,136},{16,144},{24,152},{32,160},{40,168},{48,176},{56,1... | collective-permute-start | bytes 153608 | tf_op jit(solution)/shard_map/ppermute | solution.py:13
  290.6 8.5 %collective-permute-start.11 = (bf16[1,10,10,256]{3,2,1,0:T(8,128)(2,1)S(1)}, bf16[1,10,10,256]{3,2,1,0:T(8,128)(2,1)S(1)}, u32[]{:S(2)}, u32[]{:S(2)}) collective-permute-start(bf16[1,10,10,256]{3,2,1,0:T(8,128)(2,1)S(1)} %get-tuple-element.6), channel_id=1, source_target_pairs={{128,0},{136,8},{144,16},{152,24},{160,32},{168,40},{176,48},{184,... | collective-permute-start | bytes 153608 | tf_op jit(solution)/shard_map/ppermute | solution.py:13
  299.5 5.2 %copy-start.1 = (f32[32]{0:T(128)S(1)}, f32[32]{0:T(128)}, u32[]{:S(2)}) copy-start(f32[32]{0:T(128)} %param.9) | copy-start | bytes 388
where the time goes:
time: 306 us; the launch traced here: 305 us
  blocking collectives  192 us (63%)
  starting transfers between devices  46.5 us (15%)
  waiting for transfers between devices  37.7 us (12%)
  local copies, waits for them, and re-layouts  18.9 us (6%)
  matrix products  8.1 us (3%)
    all_gather x1, blocking collectives, on_device(): lax.all_gather(padded, 'chan', axis=3, tiled=True)  100 us
    all_gather x1, blocking collectives, on_device(): whole = lax.all_gather(hidden, 'chan', axis=3, tiled=True)  80 us
    ppermute x12, starting transfers between devices, shifted(): return lax.ppermute(x, axis, pairs)  46.5 us
    ppermute x12, waiting for transfers between devices, shifted(): return lax.ppermute(x, axis, pairs)  37.7 us
    all_to_all x1, blocking collectives, on_device(): lax.all_to_all(blocks, 'chan', split_axis=4, concat_axis=0, tiled=True)  11.5 us
    conv_general_dilated x2, matrix products, convolve_valid(): lax.conv_general_dilated(padded[None], kernel, (1, 1, 1), 'VALID', dimens...  8.1 us
    broadcast_in_dim x1, local copies, waits for them, and re-layouts, convolve_valid(): padded[None]  7.52 us
  transfers between devices with their start and end apart: 12, of which 6 were waited for; matrix products, arithmetic and copies ran while one was open for 0% of the time, Pallas kernels for 0%

commit v1 on v0

v1 whole, which is shorter than its diff:
```python
import jax
import jax.numpy as jnp
import numpy as np
from jax import lax
from jax.experimental import pallas as pl
from jax.experimental.pallas import tpu as pltpu
from jax.sharding import PartitionSpec as P

MESH = pl.DeviceIdType.MESH
G = 4
PIECES = (
    ((1, 0, 0), 64, 32),
    ((0, 1, 0), 96, 32),
    ((0, 0, 1), 128, 32),
    ((1, 1, 0), 160, 16),
    ((1, 0, 1), 176, 16),
    ((0, 1, 1), 192, 16),
    ((1, 1, 1), 208, 16),
)
OWN = 64
SLOT = 224
RIM = SLOT - OWN


def unpack_matrix():
    def place(n):
        if n < 2:
            return 1, True, n
        if n < 6:
            return 0, False, n - 2
        if n < 10:
            return 1, False, n - 6
        return 0, True, n - 10

    out = np.zeros((4, 3, 12, 16, 256), np.float32)
    for u in range(4):
        for shift in range(3):
            for y in range(12):
                for z in range(10):
                    b, rim_y, v = place(y)
                    c, rim_z, w = place(z + shift)
                    at = (2 * b + c) * 64
                    if rim_y and rim_z:
                        at += 48 + u * 4 + v * 2 + w
                    elif rim_z:
                        at += 32 + (u % 2) * 8 + v * 2 + w
                    elif rim_y:
                        at += 16 + (u % 2) * 8 + v * 4 + w
                    else:
                        at += v * 4 + w
                    out[u, shift, y, z, at] = 1
    return out.reshape(4, 576, 256).astype(jnp.bfloat16)


def kernel(
    x_ref, k1_hbm, b1_ref, k2_hbm, b2_ref, p_hbm, out_ref,
    land, pack, k1, k2, pick, wide, hidden, mask,
    load_sem, a_send, a_recv, b_send, b_recv, c_send, c_recv,
):
    space, chan = lax.axis_index("space"), lax.axis_index("chan")
    i, j, k = space // (G * G), space // G % G, space % G
    oct_a, oct_b, oct_c = chan // 4, chan // 2 % 2, chan % 2

    loads = [
        pltpu.make_async_copy(src, dst, load_sem.at[n])
        for n, (src, dst) in enumerate(((p_hbm, pick), (k1_hbm, k1), (k2_hbm, k2)))
    ]
    for load in loads:
        load.start()

    def tile(way, sign):
        ti = (i + sign * way[0] * (2 * oct_a - 1) + G) % G
        tj = (j + sign * way[1] * (2 * oct_b - 1) + G) % G
        tk = (k + sign * way[2] * (2 * oct_c - 1) + G) % G
        return (ti * G + tj) * G + tk

    barrier = pltpu.get_barrier_semaphore()
    for way, _, _ in PIECES:
        pl.semaphore_signal(barrier, inc=1, device_id=(tile(way, -1), chan), device_id_type=MESH)
    for d in range(1, 8):
        pl.semaphore_signal(barrier, inc=1, device_id=(space, (chan + d) % 8), device_id_type=MESH)

    x = x_ref[...]
    r = lax.broadcasted_iota(jnp.int32, (RIM, OWN), 0)
    col = lax.broadcasted_iota(jnp.int32, (RIM, OWN), 1)
    xs, ys, zs = 32 * oct_a, 8 * oct_b, 2 * oct_c
    src = jnp.full((RIM, OWN), -1, jnp.int32)
    ok_x = (i + 2 * oct_a - 1 >= 0) & (i + 2 * oct_a - 1 < G)
    ok_y = (j + 2 * oct_b - 1 >= 0) & (j + 2 * oct_b - 1 < G)
    ok_z = (k + 2 * oct_c - 1 >= 0) & (k + 2 * oct_c - 1 < G)
    for way, start, rows in PIECES:
        q = r - (start - OWN)
        at = jnp.zeros_like(r)
        if way[2]:
            at = at + zs + (q & 1)
            q = q >> 1
        else:
            at = at + (q & 3)
            q = q >> 2
        if way[1]:
            at = at + ys + 4 * (q & 1)
            q = q >> 1
        else:
            at = at + 4 * (q & 3)
            q = q >> 2
        at = at + 16 * q + (xs if way[0] else 0)
        if way == (1, 1, 1):
            rows = 8
        ok = jnp.int32(1)
        for crosses, fine in zip(way, (ok_x, ok_y, ok_z)):
            if crosses:
                ok = ok * fine.astype(jnp.int32)
        at = jnp.where(ok == 1, at, -1)
        inside = (r >= start - OWN) & (r < start - OWN + rows)
        src = jnp.where(inside, at, src)
    select = jnp.where(src == col, 1.0, 0.0).astype(jnp.bfloat16)
    pack[...] = jnp.dot(select, x, preferred_element_type=jnp.float32).astype(jnp.bfloat16)
    land[chan, 0:OWN] = x

    pl.semaphore_wait(barrier, 14)

    rims = []
    for n, (way, start, rows) in enumerate(PIECES):
        rims.append(
            pltpu.make_async_remote_copy(
                src_ref=pack.at[pl.ds(start - OWN, rows)],
                dst_ref=land.at[chan, pl.ds(start, rows)],
                send_sem=a_send.at[n],
                recv_sem=a_recv.at[n],
                device_id=(tile(way, 1), chan),
                device_id_type=MESH,
            )
        )
        rims[-1].start()
    owns, relays = [], []
    for d in range(1, 8):
        to = (space, (chan + d) % 8)
        owns.append(
            pltpu.make_async_remote_copy(
                src_ref=x_ref,
                dst_ref=land.at[chan, pl.ds(0, OWN)],
                send_sem=b_send.at[d - 1],
                recv_sem=b_recv.at[d - 1],
                device_id=to,
                device_id_type=MESH,
            )
        )
        owns[-1].start()
        relays.append(
            pltpu.make_async_remote_copy(
                src_ref=land.at[chan, pl.ds(OWN, RIM)],
                dst_ref=land.at[chan, pl.ds(OWN, RIM)],
                send_sem=c_send.at[d - 1],
                recv_sem=c_recv.at[d - 1],
                device_id=to,
                device_id_type=MESH,
            )
        )
    row = lax.broadcasted_iota(jnp.int32, (160, 256), 0)
    hy, hz = row >> 4, row & 15
    outside = ((j == 0) & (hy == 0)) | ((j == G - 1) & (hy == 9))
    outside = outside | ((k == 0) & (hz == 0)) | ((k == G - 1) & (hz == 9))
    mask[...] = jnp.where(outside, 0.0, 1.0)

    for copy in rims:
        copy.wait_recv()
    for copy in relays:
        copy.start()
    for copy in owns:
        copy.wait_recv()
    for load in loads:
        load.wait()
    for copy in relays:
        copy.wait_recv()

    def unpack(u, chunks, x_of):
        sides = []
        for a in range(2):
            parts = []
            for s in range(4):
                for chunk in chunks:
                    parts.append(land[a * 4 + s, pl.ds(pl.multiple_of(chunk, 16), 16)])
            sides.append(jnp.concatenate(parts, axis=0))
        voxels = jnp.concatenate(sides, axis=1)
        got = jnp.dot(pick[u], voxels, preferred_element_type=jnp.float32).astype(jnp.bfloat16)
        for a in range(2):
            for shift in range(3):
                piece = got[shift * 192 : (shift + 1) * 192, a * 128 : (a + 1) * 128]
                wide[x_of[a], :, :, shift * 128 : (shift + 1) * 128] = piece.reshape(12, 16, 128)

    def own_plane(u, _):
        unpack(u, (16 * u, 96 + 16 * (u // 2), 128 + 16 * (u // 2), 192), (2 + u, 6 + u))
        return 0

    def rim_plane(h, _):
        unpack(h, (64 + 16 * h, 160, 176, 208), (10 + h, h))
        return 0

    lax.fori_loop(0, 4, own_plane, 0)
    lax.fori_loop(0, 2, rim_plane, 0)

    bias_one = b1_ref[...]

    def first(n, _):
        at = 2 * n
        taps = [
            wide[pl.ds(at + a, 2), b : b + 10].reshape(320, 384) for a in range(3) for b in range(3)
        ]
        total = jnp.dot(jnp.concatenate(taps, axis=1), k1[...], preferred_element_type=jnp.float32)
        total = jnp.maximum(total + bias_one, 0.0)
        for p in range(2):
            inside = ((at + p > 0) | (i > 0)) & ((at + p < 9) | (i < G - 1))
            keep = mask[...] * jnp.where(inside, 1.0, 0.0)
            plane = total[p * 160 : (p + 1) * 160] * keep
            hidden[at + p] = plane.astype(jnp.bfloat16).reshape(10, 16, 256)
        return 0

    lax.fori_loop(0, 5, first, 0)

    bias_two = b2_ref[...]

    def second(n, _):
        at = 4 * n
        total = jnp.zeros((512, 96), jnp.float32)
        for a in range(3):
            for b in range(3):
                voxels = hidden[pl.ds(at + a, 4), b : b + 8].reshape(512, 256)
                total = total + lax.dot_general(
                    voxels, k2[3 * a + b], (((1,), (1,)), ((), ())), preferred_element_type=jnp.float32
                )
        total = total.reshape(32, 16, 96)
        result = total[:, 0:8, 0:32] + total[:, 1:9, 32:64] + total[:, 2:10, 64:96] + bias_two
        result = jnp.maximum(result, 0.0).astype(jnp.bfloat16)
        out_ref[pl.ds(pl.multiple_of(n * 32, 32), 32)] = result
        return 0

    lax.fori_loop(0, 2, second, 0)

    for copy in rims + owns + relays:
        copy.wait_send()


def on_device(blocks, kernel_one, bias_one, kernel_two, bias_two):
    cin, f1 = kernel_one.shape[3:]
    f2 = kernel_two.shape[4]
    vmem, anywhere = pl.BlockSpec(memory_space=pltpu.VMEM), pl.BlockSpec(memory_space=pl.ANY)
    dma = pltpu.SemaphoreType.DMA
    out = pl.pallas_call(
        kernel,
        out_shape=jax.ShapeDtypeStruct((64, 8, f2), jnp.bfloat16),
        in_specs=[vmem, anywhere, vmem, anywhere, vmem, anywhere],
        out_specs=vmem,
        scratch_shapes=[
            pltpu.VMEM((8, SLOT, cin), jnp.bfloat16),
            pltpu.VMEM((RIM, cin), jnp.bfloat16),
            pltpu.VMEM((27 * cin, f1), jnp.bfloat16),
            pltpu.VMEM((9, 3 * f2, f1), jnp.bfloat16),
            pltpu.VMEM((4, 576, 256), jnp.bfloat16),
            pltpu.VMEM((12, 12, 16, 3 * cin), jnp.bfloat16),
            pltpu.VMEM((10, 10, 16, f1), jnp.bfloat16),
            pltpu.VMEM((160, f1), jnp.float32),
            dma((3,)), dma((7,)), dma((7,)), dma((7,)), dma((7,)), dma((7,)), dma((7,)),
        ],
        compiler_params=pltpu.CompilerParams(
            collective_id=0, has_side_effects=True, vmem_limit_bytes=48 * 1024 * 1024
        ),
        cost_estimate=pl.CostEstimate(flops=2_000_000_000, bytes_accessed=4_000_000, transcendentals=0),
    )(
        blocks.reshape(64, cin),
        kernel_one.reshape(27 * cin, f1),
        bias_one.reshape(1, f1),
        kernel_two.transpose(0, 1, 2, 4, 3).reshape(9, 3 * f2, f1),
        bias_two.reshape(1, f2),
        jnp.asarray(unpack_matrix()),
    )
    return out.reshape(1, 8, 8, 8, f2)


def solution(mesh):
    placed = (
        P(("space", "chan"), None, None, None, None),
        P(),
        P(),
        P(None, None, None, None, "chan"),
        P("chan"),
    )
    return jax.shard_map(
        on_device,
        mesh=mesh,
        in_specs=placed,
        out_specs=P("space", None, None, None, "chan"),
        check_vma=False,
    )
```

time: 306 us -> 41.3 us (0.13)
  blocking collectives: 192 us -> 0 us
  starting transfers between devices: 46.5 us -> 0 us
  waiting for transfers between devices: 37.7 us -> 0 us
  Pallas kernels: 0 us -> 34.5 us
  local copies, waits for them, and re-layouts: 18.9 us -> 6.47 us
  matrix products: 8.1 us -> 0 us
    all_gather x2 -> x0, blocking collectives: 180 us -> none  [the longest x1 100 us: on_device(): lax.all_gather(padded, 'chan', axis=3, tiled=True)]
    ppermute x12 -> x0, starting transfers between devices: 46.5 us -> none  [shifted(): return lax.ppermute(x, axis, pairs)]
    ppermute x12 -> x0, waiting for transfers between devices: 37.7 us -> none  [shifted(): return lax.ppermute(x, axis, pairs)]
    pallas_call x0 -> x1, Pallas kernels: none -> 34.5 us  [on_device(): pl.pallas_call(kernel, out_shape=jax.ShapeDtypeStruct((64, 8, f2), jnp.bf...]
    all_to_all x1 -> x0, blocking collectives: 11.5 us -> none  [on_device(): lax.all_to_all(blocks, 'chan', split_axis=4, concat_axis=0, tiled=True)]
    conv_general_dilated x2 -> x0, matrix products: 8.1 us -> none  [convolve_valid(): lax.conv_general_dilated(padded[None], kernel, (1, 1, 1), 'VALID', dimens...]
    broadcast_in_dim x1 -> x0, local copies, waits for them, and re-layouts: 7.52 us -> none  [convolve_valid(): padded[None]]
    all_gather x1 -> x0, local copies, waits for them, and re-layouts: 4.8 us -> none  [on_device(): whole = lax.all_gather(hidden, 'chan', axis=3, tiled=True)]
  transfers between devices with their start and end apart: 12 -> 0, of which waited for: 6 -> 0; matrix products, arithmetic and copies ran while one was open for 0% -> 0% of each run, Pallas kernels for 0% -> 0%
where the time goes in v1:
time: 41.3 us; the launch traced here: 41 us
  Pallas kernels  34.5 us (84%)
  local copies, waits for them, and re-layouts  6.47 us (16%)
    pallas_call x1, Pallas kernels, on_device(): pl.pallas_call(kernel, out_shape=jax.ShapeDtypeStruct((64, 8, f2), jnp.bf...  34.5 us
    unnamed x13, local copies, waits for them, and re-layouts  6.47 us

profile of v1, /device:TPU:1, one launch (start us, length us, event | category | flops | bytes accessed | tf_op | source)
XLA Modules:
  0.0 41.0 jit_solution(16562489029265388303)
XLA Ops:
  0.0 0.0 copy-start
  0.0 1.5 %copy-done = bf16[3,3,3,128,256]{4,3,2,1,0:T(8,128)(2,1)S(1)} copy-done((bf16[3,3,3,128,256]{4,3,2,1,0:T(8,128)(2,1)S(1)}, bf16[3,3,3,128,256]{4,3,2,1,0:T(8,128)(2,1)}, u32[]{:S(2)}) %copy-start) | copy-done | bytes 1769496
  1.5 0.0 copy-start.1
  1.5 1.0 %copy-done.1 = bf16[3,3,3,256,32]{3,4,2,1,0:T(8,128)(2,1)S(1)} copy-done((bf16[3,3,3,256,32]{3,4,2,1,0:T(8,128)(2,1)S(1)}, bf16[3,3,3,256,32]{3,4,2,1,0:T(8,128)(2,1)}, u32[]{:S(2)}) %copy-start.1) | copy-done | bytes 442392
  2.5 0.0 copy-start.2
  2.5 0.7 %copy-done.2 = bf16[1,4,4,4,128]{4,3,2,1,0:T(4,128)(2,1)S(1)} copy-done((bf16[1,4,4,4,128]{4,3,2,1,0:T(4,128)(2,1)S(1)}, bf16[1,4,4,4,128]{4,3,2,1,0:T(4,128)(2,1)}, u32[]{:S(2)}) %copy-start.2) | copy-done | bytes 16408
  3.2 0.0 copy-start.3
  3.2 0.7 %copy-done.3 = f32[256]{0:T(256)S(1)} copy-done((f32[256]{0:T(256)S(1)}, f32[256]{0:T(256)}, u32[]{:S(2)}) %copy-start.3) | copy-done | bytes 1048
  3.9 0.0 copy-start.4
  3.9 0.7 %copy-done.4 = f32[32]{0:T(128)S(1)} copy-done((f32[32]{0:T(128)S(1)}, f32[32]{0:T(128)}, u32[]{:S(2)}) %copy-start.4) | copy-done | bytes 152
  4.5 0.0 copy-start.5
  4.5 1.3 %copy-done.5 = bf16[4,576,256]{2,1,0:T(8,128)(2,1)S(1)} copy-done((bf16[4,576,256]{2,1,0:T(8,128)(2,1)S(1)}, bf16[4,576,256]{2,1,0:T(8,128)(2,1)}, u32[]{:S(2)}) %copy-start.5) | copy-done | bytes 1179672
  5.8 34.5 %shard_map.64 = bf16[64,8,32]{2,1,0:T(8,128)(2,1)S(1)} custom-call(bf16[64,128]{1,0:T(8,128)(2,1)S(1)} %bitcast.11, bf16[3456,256]{1,0:T(8,128)(2,1)S(1)} %bitcast.9, f32[1,256]{1,0:T(1,128)S(1)} %bitcast.12, bf16[9,96,256]{2,1,0:T(8,128)(2,1)S(1)} %bitcast.10, f32[1,32]{1,0:T(1,128)S(1)} %bitcast.13, bf16[4,576,256]{2,1,0:T(8,128)(2,1)S(1)} %copy-done.5), custom_call_target="tpu_custom_call" | custom-call | flops 2000000000 | bytes 4000000 | tf_op jit(solution)/shard_map/pallas_call | solution.py:248
  40.3 0.7 %copy.8 = bf16[1,8,8,8,32]{4,3,2,1,0:T(8,128)(2,1)} copy(bf16[1,8,8,8,32]{4,3,2,1,0:T(8,128)(2,1)S(1)} %bitcast.8) | data formatting | bytes 65536
Async XLA Ops:
  0.0 1.5 %copy-start = (bf16[3,3,3,128,256]{4,3,2,1,0:T(8,128)(2,1)S(1)}, bf16[3,3,3,128,256]{4,3,2,1,0:T(8,128)(2,1)}, u32[]{:S(2)}) copy-start(bf16[3,3,3,128,256]{4,3,2,1,0:T(8,128)(2,1)} %param.7) | copy-start | bytes 5308420
  1.5 1.0 %copy-start.1 = (bf16[3,3,3,256,32]{3,4,2,1,0:T(8,128)(2,1)S(1)}, bf16[3,3,3,256,32]{3,4,2,1,0:T(8,128)(2,1)}, u32[]{:S(2)}) copy-start(bf16[3,3,3,256,32]{3,4,2,1,0:T(8,128)(2,1)} %param.9) | copy-start | bytes 1327108
  2.5 0.7 %copy-start.2 = (bf16[1,4,4,4,128]{4,3,2,1,0:T(4,128)(2,1)S(1)}, bf16[1,4,4,4,128]{4,3,2,1,0:T(4,128)(2,1)}, u32[]{:S(2)}) copy-start(bf16[1,4,4,4,128]{4,3,2,1,0:T(4,128)(2,1)} %param.6) | copy-start | bytes 49156
  3.2 0.7 %copy-start.3 = (f32[256]{0:T(256)S(1)}, f32[256]{0:T(256)}, u32[]{:S(2)}) copy-start(f32[256]{0:T(256)} %param.8) | copy-start | bytes 3076
  3.9 0.7 %copy-start.4 = (f32[32]{0:T(128)S(1)}, f32[32]{0:T(128)}, u32[]{:S(2)}) copy-start(f32[32]{0:T(128)} %param.10) | copy-start | bytes 388
  4.5 1.3 %copy-start.5 = (bf16[4,576,256]{2,1,0:T(8,128)(2,1)S(1)}, bf16[4,576,256]{2,1,0:T(8,128)(2,1)}, u32[]{:S(2)}) copy-start(bf16[4,576,256]{2,1,0:T(8,128)(2,1)} %constant.2.clone.p_hbm) | copy-start | bytes 3538948

commit v2 on v1

v2 whole, which is shorter than its diff:
```python
import jax
import jax.numpy as jnp
import numpy as np
from jax import lax
from jax.experimental import pallas as pl
from jax.experimental.pallas import tpu as pltpu
from jax.sharding import PartitionSpec as P

MESH = pl.DeviceIdType.MESH
G = 4
PIECES = (
    ((0, 0, 1), 64, 32),
    ((1, 0, 0), 96, 32),
    ((1, 0, 1), 128, 16),
    ((0, 1, 0), 144, 32),
    ((0, 1, 1), 176, 16),
    ((1, 1, 0), 192, 16),
    ((1, 1, 1), 208, 16),
)
NEAR = 3
OWN = 64
SLOT = 224
RIM = SLOT - OWN
HALF = RIM // 2


def unpack_matrices():
    def place(n):
        if n < 2:
            return 1, n
        return (1, n - 6) if n >= 6 and n < 10 else (0, (n - 2) % 8)

    inner = np.zeros((2, 3, 8, 16, 128), np.float32)
    outer = np.zeros((4, 3, 4, 16, 128), np.float32)
    for shift in range(3):
        for z in range(10):
            c, w = place(z + shift)
            rim = z + shift < 2 or z + shift >= 10
            for u in range(2):
                for y in range(8):
                    at = (2 * (y // 4) + c) * 32
                    v = y % 4
                    inner[u, shift, y, z, at + (16 + u * 8 + v * 2 + w if rim else v * 4 + w)] = 1
            for u in range(4):
                for y in range(4):
                    at = (2 * (1 - y // 2) + c) * 32
                    v = y % 2
                    outer[u, shift, y, z, at + (16 + u * 4 + v * 2 + w if rim else (u % 2) * 8 + v * 4 + w)] = 1
    return inner.reshape(2, 384, 128).astype(jnp.bfloat16), outer.reshape(4, 192, 128).astype(jnp.bfloat16)


def kernel(
    x_hbm, k1_hbm, b1_hbm, k2_hbm, b2_hbm, p_hbm, q_hbm, out_ref,
    x_ref, b1_ref, b2_ref, land, pack, k1, k2, k2_t, pick, pick_rim, wide, hidden, mask,
    load_sem, a_send, a_recv, b_send, b_recv, c_send, c_recv, d_send, d_recv,
):
    space, chan = lax.axis_index("space"), lax.axis_index("chan")
    i, j, k = space // (G * G), space // G % G, space % G
    oct_a, oct_b, oct_c = chan // 4, chan // 2 % 2, chan % 2

    def tile(way, sign):
        ti = (i + sign * way[0] * (2 * oct_a - 1) + G) % G
        tj = (j + sign * way[1] * (2 * oct_b - 1) + G) % G
        tk = (k + sign * way[2] * (2 * oct_c - 1) + G) % G
        return (ti * G + tj) * G + tk

    barrier = pltpu.get_barrier_semaphore()
    for way, _, _ in PIECES[::-1]:
        pl.semaphore_signal(barrier, inc=1, device_id=(tile(way, -1), chan), device_id_type=MESH)
    for d in range(1, 8):
        pl.semaphore_signal(barrier, inc=1, device_id=(space, (chan + d) % 8), device_id_type=MESH)

    pairs = (x_hbm, x_ref), (p_hbm, pick), (q_hbm, pick_rim), (k1_hbm, k1), (k2_hbm, k2), (b1_hbm, b1_ref), (b2_hbm, b2_ref)
    loads = [
        pltpu.make_async_copy(src, dst, load_sem.at[n]) for n, (src, dst) in enumerate(pairs)
    ]
    for load in loads:
        load.start()

    r = lax.broadcasted_iota(jnp.int32, (RIM, OWN), 0)
    col = lax.broadcasted_iota(jnp.int32, (RIM, OWN), 1)
    xs, ys, zs = 32 * oct_a, 8 * oct_b, 2 * oct_c
    src = jnp.full((RIM, OWN), -1, jnp.int32)
    ok_x = (i + 2 * oct_a - 1 >= 0) & (i + 2 * oct_a - 1 < G)
    ok_y = (j + 2 * oct_b - 1 >= 0) & (j + 2 * oct_b - 1 < G)
    ok_z = (k + 2 * oct_c - 1 >= 0) & (k + 2 * oct_c - 1 < G)
    for way, start, rows in PIECES:
        q = r - (start - OWN)
        at = jnp.zeros_like(r)
        if way[2]:
            at = at + zs + (q & 1)
            q = q >> 1
        else:
            at = at + (q & 3)
            q = q >> 2
        if way[1]:
            at = at + ys + 4 * (q & 1)
            q = q >> 1
        else:
            at = at + 4 * (q & 3)
            q = q >> 2
        at = at + 16 * q + (xs if way[0] else 0)
        if way == (1, 1, 1):
            rows = 8
        ok = jnp.int32(1)
        for crosses, fine in zip(way, (ok_x, ok_y, ok_z)):
            if crosses:
                ok = ok * fine.astype(jnp.int32)
        at = jnp.where(ok == 1, at, -1)
        inside = (r >= start - OWN) & (r < start - OWN + rows)
        src = jnp.where(inside, at, src)
    loads[0].wait()
    x = x_ref[...]
    select = jnp.where(src == col, 1.0, 0.0).astype(jnp.bfloat16)
    pack[...] = jnp.dot(select, x, preferred_element_type=jnp.float32).astype(jnp.bfloat16)
    land[chan, 0:OWN] = x

    pl.semaphore_wait(barrier, 14)

    rims = []
    for n, (way, start, rows) in enumerate(PIECES):
        rims.append(
            pltpu.make_async_remote_copy(
                src_ref=pack.at[pl.ds(start - OWN, rows)],
                dst_ref=land.at[chan, pl.ds(start, rows)],
                send_sem=a_send.at[n],
                recv_sem=a_recv.at[n],
                device_id=(tile(way, 1), chan),
                device_id_type=MESH,
            )
        )
    for copy in rims[::-1]:
        copy.start()

    def to_tile(src_of, start, rows, send_sem, recv_sem):
        return [
            pltpu.make_async_remote_copy(
                src_ref=src_of,
                dst_ref=land.at[chan, pl.ds(start, rows)],
                send_sem=send_sem.at[d - 1],
                recv_sem=recv_sem.at[d - 1],
                device_id=(space, (chan + d) % 8),
                device_id_type=MESH,
            )
            for d in range(1, 8)
        ]

    owns = to_tile(x_ref, 0, OWN, b_send, b_recv)
    near = to_tile(land.at[chan, pl.ds(OWN, HALF)], OWN, HALF, c_send, c_recv)
    far = to_tile(land.at[chan, pl.ds(OWN + HALF, HALF)], OWN + HALF, HALF, d_send, d_recv)
    for copy in owns:
        copy.start()

    row = lax.broadcasted_iota(jnp.int32, (160, 256), 0)
    hy, hz = row >> 4, row & 15
    outside = ((j == 0) & (hy == 0)) | ((j == G - 1) & (hy == 9))
    outside = outside | ((k == 0) & (hz == 0)) | ((k == G - 1) & (hz == 9))
    mask[...] = jnp.where(outside, 0.0, 1.0).reshape(10, 16, 256)
    for load in loads[1:]:
        load.wait()
    for n in range(9):
        k2_t[n * 256 : (n + 1) * 256, :] = k2[n].T

    for copy in rims[:NEAR]:
        copy.wait_recv()
    for copy in near:
        copy.start()
    for copy in rims[NEAR:]:
        copy.wait_recv()
    for copy in far:
        copy.start()
    for copy in owns:
        copy.wait_recv()
    for copy in near:
        copy.wait_recv()

    def unpack(matrix, chunks, x_of, y_of):
        sides = []
        for a in range(2):
            parts = []
            for s in range(4):
                for chunk in chunks:
                    parts.append(land[a * 4 + s, chunk : chunk + 16])
            sides.append(jnp.concatenate(parts, axis=0))
        voxels = jnp.concatenate(sides, axis=1)
        got = jnp.dot(matrix, voxels, preferred_element_type=jnp.float32).astype(jnp.bfloat16)
        rows = got.shape[0] // 3
        for a in range(2):
            for shift in range(3):
                piece = got[shift * rows : (shift + 1) * rows, a * 128 : (a + 1) * 128]
                piece = piece.reshape(rows // 16, 16, 128)
                at = 0
                for y, count in y_of:
                    wide[x_of[a], y : y + count, :, shift * 128 : (shift + 1) * 128] = piece[at : at + count]
                    at += count

    bias_one, bias_two = b1_ref[...], b2_ref[...]

    def stack(ref, at, planes, shift, y_of):
        parts = [ref[at : at + planes, y + shift : y + shift + count] for y, count in y_of]
        whole = jnp.concatenate(parts, axis=1) if len(parts) > 1 else parts[0]
        return whole.reshape(-1, whole.shape[3])

    def first(at, planes, y_of):
        taps = [stack(wide, at + a, planes, b, y_of) for a in range(3) for b in range(3)]
        total = jnp.dot(jnp.concatenate(taps, axis=1), k1[...], preferred_element_type=jnp.float32)
        total = jnp.maximum(total + bias_one, 0.0).reshape(planes, -1, 16, 256)
        for p in range(planes):
            inside = ((at + p > 0) | (i > 0)) & ((at + p < 9) | (i < G - 1))
            keep = jnp.where(inside, 1.0, 0.0)
            row = 0
            for y, count in y_of:
                plane = total[p, row : row + count] * (mask[y : y + count] * keep)
                hidden[at + p, y : y + count] = plane.astype(jnp.bfloat16)
                row += count

    def second(at, planes, y_of):
        taps = [stack(hidden, at + a, planes, b, y_of) for a in range(3) for b in range(3)]
        total = jnp.dot(jnp.concatenate(taps, axis=1), k2_t[...], preferred_element_type=jnp.float32)
        total = total.reshape(-1, 16, 96)
        result = total[:, 0:8, 0:32] + total[:, 1:9, 32:64] + total[:, 2:10, 64:96] + bias_two
        result = jnp.maximum(result, 0.0).astype(jnp.bfloat16).reshape(planes, -1, 8, 32)
        row = 0
        for y, count in y_of:
            out_ref[at : at + planes, y : y + count] = result[:, row : row + count]
            row += count

    def inner(p):
        for n in range(2):
            u = p + 2 * n
            unpack(pick[p], (16 * u, 64 + 16 * n), (2 + u, 6 + u), ((2, 8),))
        unpack(pick[p], (96 + 16 * p, 128), (10 + p, p), ((2, 8),))

    def outer(p):
        for n in range(2):
            u = p + 2 * n
            unpack(pick_rim[u], (144 + 16 * n, 176), (2 + u, 6 + u), ((0, 2), (10, 2)))
        unpack(pick_rim[p], (192, 208), (10 + p, p), ((0, 2), (10, 2)))

    inner(0)
    inner(1)
    first(0, 5, ((2, 6),))
    first(5, 5, ((2, 6),))
    second(0, 4, ((2, 4),))
    second(4, 4, ((2, 4),))

    for copy in far:
        copy.wait_recv()
    outer(0)
    outer(1)
    first(0, 5, ((0, 2), (8, 2)))
    first(5, 5, ((0, 2), (8, 2)))
    second(0, 4, ((0, 2), (6, 2)))
    second(4, 4, ((0, 2), (6, 2)))

    for copy in rims + owns + near + far:
        copy.wait_send()


def on_device(blocks, kernel_one, bias_one, kernel_two, bias_two):
    cin, f1 = kernel_one.shape[3:]
    f2 = kernel_two.shape[4]
    vmem, hbm = pl.BlockSpec(memory_space=pltpu.VMEM), pl.BlockSpec(memory_space=pltpu.HBM)
    dma = pltpu.SemaphoreType.DMA
    out = pl.pallas_call(
        kernel,
        out_shape=jax.ShapeDtypeStruct((8, 8, 8, f2), jnp.bfloat16),
        in_specs=[hbm] * 7,
        out_specs=vmem,
        scratch_shapes=[
            pltpu.VMEM((OWN, cin), jnp.bfloat16),
            pltpu.VMEM((1, f1), jnp.float32),
            pltpu.VMEM((1, f2), jnp.float32),
            pltpu.VMEM((8, SLOT, cin), jnp.bfloat16),
            pltpu.VMEM((RIM, cin), jnp.bfloat16),
            pltpu.VMEM((27 * cin, f1), jnp.bfloat16),
            pltpu.VMEM((9, 3 * f2, f1), jnp.bfloat16),
            pltpu.VMEM((9 * f1, 3 * f2), jnp.bfloat16),
            pltpu.VMEM((2, 384, 128), jnp.bfloat16),
            pltpu.VMEM((4, 192, 128), jnp.bfloat16),
            pltpu.VMEM((12, 12, 16, 3 * cin), jnp.bfloat16),
            pltpu.VMEM((10, 10, 16, f1), jnp.bfloat16),
            pltpu.VMEM((10, 16, f1), jnp.float32),
            dma((7,)), dma((7,)), dma((7,)), dma((7,)), dma((7,)), dma((7,)), dma((7,)), dma((7,)), dma((7,)),
        ],
        compiler_params=pltpu.CompilerParams(
            collective_id=0, has_side_effects=True, vmem_limit_bytes=64 * 1024 * 1024
        ),
        cost_estimate=pl.CostEstimate(flops=2_000_000_000, bytes_accessed=4_000_000, transcendentals=0),
    )(
        blocks.reshape(64, cin),
        kernel_one.reshape(27 * cin, f1),
        bias_one.reshape(1, f1),
        kernel_two.transpose(0, 1, 2, 4, 3).reshape(9, 3 * f2, f1),
        bias_two.reshape(1, f2),
        *(jnp.asarray(matrix) for matrix in unpack_matrices()),
    )
    return out.reshape(1, 8, 8, 8, f2)


def solution(mesh):
    placed = (
        P(("space", "chan"), None, None, None, None),
        P(),
        P(),
        P(None, None, None, None, "chan"),
        P("chan"),
    )
    return jax.shard_map(
        on_device,
        mesh=mesh,
        in_specs=placed,
        out_specs=P("space", None, None, None, "chan"),
        check_vma=False,
    )
```

time: 41.3 us -> 32.7 us (0.79)
  local copies, waits for them, and re-layouts: 6.47 us -> 1.57 us
  Pallas kernels: 34.5 us -> 31 us
    unnamed x13 -> x1, local copies, waits for them, and re-layouts: 6.47 us -> 1.57 us
    pallas_call x1, Pallas kernels: 34.5 us -> 31 us  [on_device(): pl.pallas_call(kernel, out_shape=jax.ShapeDtypeStruct((8, 8, 8, f2), jnp....]
where the time goes in v2:
time: 32.7 us; the launch traced here: 32.5 us
  Pallas kernels  31 us (95%)
  local copies, waits for them, and re-layouts  1.57 us (5%)
    pallas_call x1, Pallas kernels, on_device(): pl.pallas_call(kernel, out_shape=jax.ShapeDtypeStruct((8, 8, 8, f2), jnp....  31 us
    unnamed x1, local copies, waits for them, and re-layouts  1.57 us

profile of v2, /device:TPU:1, one launch (start us, length us, event | category | flops | bytes accessed | tf_op | source)
XLA Modules:
  0.0 32.5 jit_solution(4785488315595091698)
XLA Ops:
  0.0 31.0 %shard_map.73 = bf16[8,8,8,32]{3,2,1,0:T(8,128)(2,1)} custom-call(bf16[64,128]{1,0:T(8,128)(2,1)} %bitcast.11, bf16[3456,256]{1,0:T(8,128)(2,1)} %bitcast.9, f32[1,256]{1,0:T(1,128)} %bitcast.12, bf16[9,96,256]{2,1,0:T(8,128)(2,1)} %bitcast.10, f32[1,32]{1,0:T(1,128)} %bitcast.13, bf16[2,384,128]{2,1,0:T(8,128)(2,1)} %constant.4.clone.p_hbm, ...), custom_call_target="tpu_custom_call" | custom-call | flops 2000000000 | bytes 4000000 | tf_op jit(solution)/shard_map/pallas_call | solution.py:265
  31.0 1.6 %copy.9 = bf16[1,8,8,8,32]{4,3,2,1,0:T(8,128)(2,1)} copy(bf16[1,8,8,8,32]{4,3,2,1,0:T(8,128)(2,1)} %bitcast.8) | data formatting | bytes 65536

commit v3 on v2

--- a/solution.py
+++ b/solution.py
@@ -64,9 +64,25 @@
         tk = (k + sign * way[2] * (2 * oct_c - 1) + G) % G
         return (ti * G + tj) * G + tk
 
+    def exists(way, sign):
+        found = True
+        for crosses, at, bit in zip(way, (i, j, k), (oct_a, oct_b, oct_c)):
+            if crosses:
+                to = at + sign * (2 * bit - 1)
+                found = (to >= 0) & (to < G) & found
+        return found
+
+    gives = [exists(way, 1) for way, _, _ in PIECES]
+    takes = [exists(way, -1) for way, _, _ in PIECES]
+
     barrier = pltpu.get_barrier_semaphore()
-    for way, _, _ in PIECES[::-1]:
-        pl.semaphore_signal(barrier, inc=1, device_id=(tile(way, -1), chan), device_id_type=MESH)
+    for n in reversed(range(7)):
+
+        @pl.when(takes[n])
+        def _():
+            to = (tile(PIECES[n][0], -1), chan)
+            pl.semaphore_signal(barrier, inc=1, device_id=to, device_id_type=MESH)
+
     for d in range(1, 8):
         pl.semaphore_signal(barrier, inc=1, device_id=(space, (chan + d) % 8), device_id_type=MESH)
 
@@ -81,9 +97,6 @@
     col = lax.broadcasted_iota(jnp.int32, (RIM, OWN), 1)
     xs, ys, zs = 32 * oct_a, 8 * oct_b, 2 * oct_c
     src = jnp.full((RIM, OWN), -1, jnp.int32)
-    ok_x = (i + 2 * oct_a - 1 >= 0) & (i + 2 * oct_a - 1 < G)
-    ok_y = (j + 2 * oct_b - 1 >= 0) & (j + 2 * oct_b - 1 < G)
-    ok_z = (k + 2 * oct_c - 1 >= 0) & (k + 2 * oct_c - 1 < G)
     for way, start, rows in PIECES:
         q = r - (start - OWN)
         at = jnp.zeros_like(r)
@@ -102,11 +115,6 @@
         at = at + 16 * q + (xs if way[0] else 0)
         if way == (1, 1, 1):
             rows = 8
-        ok = jnp.int32(1)
-        for crosses, fine in zip(way, (ok_x, ok_y, ok_z)):
-            if crosses:
-                ok = ok * fine.astype(jnp.int32)
-        at = jnp.where(ok == 1, at, -1)
         inside = (r >= start - OWN) & (r < start - OWN + rows)
         src = jnp.where(inside, at, src)
     loads[0].wait()
@@ -115,7 +123,13 @@
     pack[...] = jnp.dot(select, x, preferred_element_type=jnp.float32).astype(jnp.bfloat16)
     land[chan, 0:OWN] = x
 
-    pl.semaphore_wait(barrier, 14)
+    for n, (_, start, rows) in enumerate(PIECES):
+
+        @pl.when(~takes[n])
+        def _():
+            land[chan, start : start + rows] = jnp.zeros((rows, 128), jnp.bfloat16)
+
+    pl.semaphore_wait(barrier, 7 + sum(give.astype(jnp.int32) for give in gives))
 
     rims = []
     for n, (way, start, rows) in enumerate(PIECES):
@@ -129,8 +143,8 @@
                 device_id_type=MESH,
             )
         )
-    for copy in rims[::-1]:
-        copy.start()
+    for n in reversed(range(7)):
+        pl.when(gives[n])(rims[n].start)
 
     def to_tile(src_of, start, rows, send_sem, recv_sem):
         return [
@@ -161,12 +175,12 @@
     for n in range(9):
         k2_t[n * 256 : (n + 1) * 256, :] = k2[n].T
 
-    for copy in rims[:NEAR]:
-        copy.wait_recv()
+    for n in range(NEAR):
+        pl.when(takes[n])(rims[n].wait_recv)
     for copy in near:
         copy.start()
-    for copy in rims[NEAR:]:
-        copy.wait_recv()
+    for n in range(NEAR, 7):
+        pl.when(takes[n])(rims[n].wait_recv)
     for copy in far:
         copy.start()
     for copy in owns:
@@ -253,7 +267,9 @@
     second(0, 4, ((0, 2), (6, 2)))
     second(4, 4, ((0, 2), (6, 2)))
 
-    for copy in rims + owns + near + far:
+    for n in range(7):
+        pl.when(gives[n])(rims[n].wait_send)
+    for copy in owns + near + far:
         copy.wait_send()
 
 

time: 32.7 us -> 30.9 us (0.945)
  the two profiles are of different devices: /device:TPU:1 before, /device:TPU:41 now
where the time goes in v3:
time: 30.9 us; the launch traced here: 30.7 us
  Pallas kernels  29.1 us (94%)
  local copies, waits for them, and re-layouts  1.57 us (5%)
    pallas_call x1, Pallas kernels, on_device(): pl.pallas_call(kernel, out_shape=jax.ShapeDtypeStruct((8, 8, 8, f2), jnp....  29.1 us
    unnamed x1, local copies, waits for them, and re-layouts  1.57 us

profile of v3, /device:TPU:41, one launch (start us, length us, event | category | flops | bytes accessed | tf_op | source)
XLA Modules:
  0.0 30.7 jit_solution(3850499273153811343)
XLA Ops:
  0.0 29.1 %shard_map.73 = bf16[8,8,8,32]{3,2,1,0:T(8,128)(2,1)} custom-call(bf16[64,128]{1,0:T(8,128)(2,1)} %bitcast.11, bf16[3456,256]{1,0:T(8,128)(2,1)} %bitcast.9, f32[1,256]{1,0:T(1,128)} %bitcast.12, bf16[9,96,256]{2,1,0:T(8,128)(2,1)} %bitcast.10, f32[1,32]{1,0:T(1,128)} %bitcast.13, bf16[2,384,128]{2,1,0:T(8,128)(2,1)} %constant.4.clone.p_hbm, ...), custom_call_target="tpu_custom_call" | custom-call | flops 2000000000 | bytes 4000000 | tf_op jit(solution)/shard_map/pallas_call | solution.py:281
  29.1 1.6 %copy.9 = bf16[1,8,8,8,32]{4,3,2,1,0:T(8,128)(2,1)} copy(bf16[1,8,8,8,32]{4,3,2,1,0:T(8,128)(2,1)} %bitcast.8) | data formatting | bytes 65536

commit v4 on v3

--- a/solution.py
+++ b/solution.py
@@ -52,7 +52,7 @@
 def kernel(
     x_hbm, k1_hbm, b1_hbm, k2_hbm, b2_hbm, p_hbm, q_hbm, out_ref,
     x_ref, b1_ref, b2_ref, land, pack, k1, k2, k2_t, pick, pick_rim, wide, hidden, mask,
-    load_sem, a_send, a_recv, b_send, b_recv, c_send, c_recv, d_send, d_recv,
+    load_sem, a_send, a_recv, b_send, b_recv, c_send, c_recv, d_send, d_recv, ready,
 ):
     space, chan = lax.axis_index("space"), lax.axis_index("chan")
     i, j, k = space // (G * G), space // G % G, space % G
@@ -75,12 +75,22 @@
     gives = [exists(way, 1) for way, _, _ in PIECES]
     takes = [exists(way, -1) for way, _, _ in PIECES]
 
+    def level(tile_at):
+        return tile_at // 2 % 4
+
+    later = [level(tile(way, 1)) > level(space) for way, _, _ in PIECES]
+    earlier = [level(tile(way, -1)) < level(space) for way, _, _ in PIECES]
     barrier = pltpu.get_barrier_semaphore()
     for n in reversed(range(7)):
 
-        @pl.when(takes[n])
+        @pl.when(takes[n] & ~earlier[n])
         def _():
             to = (tile(PIECES[n][0], -1), chan)
+            pl.semaphore_signal(barrier, inc=1, device_id=to, device_id_type=MESH)
+
+        @pl.when(gives[n] & later[n])
+        def _():
+            to = (tile(PIECES[n][0], 1), chan)
             pl.semaphore_signal(barrier, inc=1, device_id=to, device_id_type=MESH)
 
     for d in range(1, 8):
@@ -129,7 +139,15 @@
         def _():
             land[chan, start : start + rows] = jnp.zeros((rows, 128), jnp.bfloat16)
 
-    pl.semaphore_wait(barrier, 7 + sum(give.astype(jnp.int32) for give in gives))
+    greeted = [g & ~late for g, late in zip(gives, later)] + [t & early for t, early in zip(takes, earlier)]
+    pl.semaphore_wait(barrier, 7 + sum(one.astype(jnp.int32) for one in greeted))
+    for n in reversed(range(7)):
+
+        @pl.when(takes[n] & earlier[n])
+        def _():
+            to = (tile(PIECES[n][0], -1), chan)
+            pl.semaphore_signal(ready.at[n], inc=1, device_id=to, device_id_type=MESH)
+
 
     rims = []
     for n, (way, start, rows) in enumerate(PIECES):
@@ -144,7 +162,7 @@
             )
         )
     for n in reversed(range(7)):
-        pl.when(gives[n])(rims[n].start)
+        pl.when(gives[n] & ~later[n])(rims[n].start)
 
     def to_tile(src_of, start, rows, send_sem, recv_sem):
         return [
@@ -179,6 +197,13 @@
         pl.when(takes[n])(rims[n].wait_recv)
     for copy in near:
         copy.start()
+    for n in (0, 2, 3, 5, 4, 6):
+
+        @pl.when(gives[n] & later[n])
+        def _():
+            pl.semaphore_wait(ready.at[n], 1)
+            rims[n].start()
+
     for n in range(NEAR, 7):
         pl.when(takes[n])(rims[n].wait_recv)
     for copy in far:
@@ -297,7 +322,7 @@
             pltpu.VMEM((12, 12, 16, 3 * cin), jnp.bfloat16),
             pltpu.VMEM((10, 10, 16, f1), jnp.bfloat16),
             pltpu.VMEM((10, 16, f1), jnp.float32),
-            dma((7,)), dma((7,)), dma((7,)), dma((7,)), dma((7,)), dma((7,)), dma((7,)), dma((7,)), dma((7,)),
+            dma((7,)), dma((7,)), dma((7,)), dma((7,)), dma((7,)), dma((7,)), dma((7,)), dma((7,)), dma((7,)), pltpu.SemaphoreType.REGULAR((7,)),
         ],
         compiler_params=pltpu.CompilerParams(
             collective_id=0, has_side_effects=True, vmem_limit_bytes=64 * 1024 * 1024

time: 30.9 us -> 27.5 us (0.89)
  the two profiles are of different devices: /device:TPU:41 before, /device:TPU:1 now
where the time goes in v4:
time: 27.5 us; the launch traced here: 27.1 us
  Pallas kernels  25.5 us (93%)
  local copies, waits for them, and re-layouts  1.57 us (6%)
    pallas_call x1, Pallas kernels, on_device(): pl.pallas_call(kernel, out_shape=jax.ShapeDtypeStruct((8, 8, 8, f2), jnp....  25.5 us
    unnamed x1, local copies, waits for them, and re-layouts  1.57 us

profile of v4, /device:TPU:1, one launch (start us, length us, event | category | flops | bytes accessed | tf_op | source)
XLA Modules:
  0.0 27.1 jit_solution(4479751834117800040)
XLA Ops:
  0.0 25.5 %shard_map.73 = bf16[8,8,8,32]{3,2,1,0:T(8,128)(2,1)} custom-call(bf16[64,128]{1,0:T(8,128)(2,1)} %bitcast.11, bf16[3456,256]{1,0:T(8,128)(2,1)} %bitcast.9, f32[1,256]{1,0:T(1,128)} %bitcast.12, bf16[9,96,256]{2,1,0:T(8,128)(2,1)} %bitcast.10, f32[1,32]{1,0:T(1,128)} %bitcast.13, bf16[2,384,128]{2,1,0:T(8,128)(2,1)} %constant.4.clone.p_hbm, ...), custom_call_target="tpu_custom_call" | custom-call | flops 2000000000 | bytes 4000000 | tf_op jit(solution)/shard_map/pallas_call | solution.py:306
  25.5 1.6 %copy.9 = bf16[1,8,8,8,32]{4,3,2,1,0:T(8,128)(2,1)} copy(bf16[1,8,8,8,32]{4,3,2,1,0:T(8,128)(2,1)} %bitcast.8) | data formatting | bytes 65536

commit v5 on v4

--- a/solution.py
+++ b/solution.py
@@ -55,6 +55,13 @@
     load_sem, a_send, a_recv, b_send, b_recv, c_send, c_recv, d_send, d_recv, ready,
 ):
     space, chan = lax.axis_index("space"), lax.axis_index("chan")
+    pairs = (x_hbm, x_ref), (p_hbm, pick), (q_hbm, pick_rim), (k1_hbm, k1), (k2_hbm, k2), (b1_hbm, b1_ref), (b2_hbm, b2_ref)
+    loads = [
+        pltpu.make_async_copy(src, dst, load_sem.at[n]) for n, (src, dst) in enumerate(pairs)
+    ]
+    for load in loads:
+        load.start()
+
     i, j, k = space // (G * G), space // G % G, space % G
     oct_a, oct_b, oct_c = chan // 4, chan // 2 % 2, chan % 2
 
@@ -95,13 +102,6 @@
 
     for d in range(1, 8):
         pl.semaphore_signal(barrier, inc=1, device_id=(space, (chan + d) % 8), device_id_type=MESH)
-
-    pairs = (x_hbm, x_ref), (p_hbm, pick), (q_hbm, pick_rim), (k1_hbm, k1), (k2_hbm, k2), (b1_hbm, b1_ref), (b2_hbm, b2_ref)
-    loads = [
-        pltpu.make_async_copy(src, dst, load_sem.at[n]) for n, (src, dst) in enumerate(pairs)
-    ]
-    for load in loads:
-        load.start()
 
     r = lax.broadcasted_iota(jnp.int32, (RIM, OWN), 0)
     col = lax.broadcasted_iota(jnp.int32, (RIM, OWN), 1)
@@ -183,6 +183,13 @@
     for copy in owns:
         copy.start()
 
+    for n in range(NEAR):
+
+        @pl.when(gives[n] & later[n])
+        def _():
+            pl.semaphore_wait(ready.at[n], 1)
+            rims[n].start()
+
     row = lax.broadcasted_iota(jnp.int32, (160, 256), 0)
     hy, hz = row >> 4, row & 15
     outside = ((j == 0) & (hy == 0)) | ((j == G - 1) & (hy == 9))
@@ -197,7 +204,7 @@
         pl.when(takes[n])(rims[n].wait_recv)
     for copy in near:
         copy.start()
-    for n in (0, 2, 3, 5, 4, 6):
+    for n in (3, 5, 4, 6):
 
         @pl.when(gives[n] & later[n])
         def _():

time: 27.5 us -> 27.5 us (level)
  no operation moved by 1% of the time
where the time goes in v5:
time: 27.5 us; the launch traced here: 27.1 us
  Pallas kernels  25.5 us (93%)
  local copies, waits for them, and re-layouts  1.57 us (6%)
    pallas_call x1, Pallas kernels, on_device(): pl.pallas_call(kernel, out_shape=jax.ShapeDtypeStruct((8, 8, 8, f2), jnp....  25.5 us
    unnamed x1, local copies, waits for them, and re-layouts  1.57 us

profile of v5, /device:TPU:1, one launch (start us, length us, event | category | flops | bytes accessed | tf_op | source)
XLA Modules:
  0.0 27.1 jit_solution(15029527264616113104)
XLA Ops:
  0.0 25.5 %shard_map.73 = bf16[8,8,8,32]{3,2,1,0:T(8,128)(2,1)} custom-call(bf16[64,128]{1,0:T(8,128)(2,1)} %bitcast.11, bf16[3456,256]{1,0:T(8,128)(2,1)} %bitcast.9, f32[1,256]{1,0:T(1,128)} %bitcast.12, bf16[9,96,256]{2,1,0:T(8,128)(2,1)} %bitcast.10, f32[1,32]{1,0:T(1,128)} %bitcast.13, bf16[2,384,128]{2,1,0:T(8,128)(2,1)} %constant.4.clone.p_hbm, ...), custom_call_target="tpu_custom_call" | custom-call | flops 2000000000 | bytes 4000000 | tf_op jit(solution)/shard_map/pallas_call | solution.py:313
  25.5 1.6 %copy.9 = bf16[1,8,8,8,32]{4,3,2,1,0:T(8,128)(2,1)} copy(bf16[1,8,8,8,32]{4,3,2,1,0:T(8,128)(2,1)} %bitcast.8) | data formatting | bytes 65536

commit v6 on v5

--- a/solution.py
+++ b/solution.py
@@ -83,7 +83,8 @@
     takes = [exists(way, -1) for way, _, _ in PIECES]
 
     def level(tile_at):
-        return tile_at // 2 % 4
+        y = tile_at // 16
+        return 4 * (tile_at // 2 % 4) + y + (y == 2) - (y == 3)
 
     later = [level(tile(way, 1)) > level(space) for way, _, _ in PIECES]
     earlier = [level(tile(way, -1)) < level(space) for way, _, _ in PIECES]

time: 27.5 us -> 27.6 us (level)
  no operation moved by 1% of the time
where the time goes in v6:
time: 27.6 us; the launch traced here: 27.2 us
  Pallas kernels  25.6 us (93%)
  local copies, waits for them, and re-layouts  1.57 us (6%)
    pallas_call x1, Pallas kernels, on_device(): pl.pallas_call(kernel, out_shape=jax.ShapeDtypeStruct((8, 8, 8, f2), jnp....  25.6 us
    unnamed x1, local copies, waits for them, and re-layouts  1.57 us

profile of v6, /device:TPU:1, one launch (start us, length us, event | category | flops | bytes accessed | tf_op | source)
XLA Modules:
  0.0 27.2 jit_solution(16315612476201191940)
XLA Ops:
  0.0 25.6 %shard_map.73 = bf16[8,8,8,32]{3,2,1,0:T(8,128)(2,1)} custom-call(bf16[64,128]{1,0:T(8,128)(2,1)} %bitcast.11, bf16[3456,256]{1,0:T(8,128)(2,1)} %bitcast.9, f32[1,256]{1,0:T(1,128)} %bitcast.12, bf16[9,96,256]{2,1,0:T(8,128)(2,1)} %bitcast.10, f32[1,32]{1,0:T(1,128)} %bitcast.13, bf16[2,384,128]{2,1,0:T(8,128)(2,1)} %constant.4.clone.p_hbm, ...), custom_call_target="tpu_custom_call" | custom-call | flops 2000000000 | bytes 4000000 | tf_op jit(solution)/shard_map/pallas_call | solution.py:314
  25.6 1.6 %copy.9 = bf16[1,8,8,8,32]{4,3,2,1,0:T(8,128)(2,1)} copy(bf16[1,8,8,8,32]{4,3,2,1,0:T(8,128)(2,1)} %bitcast.8) | data formatting | bytes 65536
